TPU v7x, 256 devices: a whole 4x4x8 slice. The times are simulated.
256 devices in a mesh: wide: 32 (over y_hi, z, core), narrow: 8 (over x, y_lo).
Axes of the slice: x: 4, y: 4 (y_hi: 2, y_lo: 2; y = y_hi * 2 + y_lo), z: 8, core: 2. Of those that a mesh axis runs over, the one named last changes fastest.
Arguments:
- gradient: bfloat16 [16384, 53248], P('wide', 'narrow'), may hold values from -6 to 6
- right_panel: float32 [53248, 512], P('narrow', 'wide'), may hold values from -0.046875 to 0.046875
- left_panel: bfloat16 [16384, 1024], P('wide'), may hold values from -0.09375 to 0.09375
- second_moment: float32 [1024, 512], P('wide', 'narrow'), may hold values from 0.1 to 10
Outputs:
- moment_new: float32 [1024, 512], P('wide', 'narrow')
- step_update: float32 [1024, 512], P('wide', 'narrow')
All inputs are finite; a program needn't handle non-finite values.
Results may differ from a plain program's by a relative error of at most 0.0003.
Values sent between devices are 32-bit elements; how exact they have to be, the bound alone decides.
A program may use at most 64 MiB of HBM per device.

v0:
```python
import jax
import jax.numpy as jnp
from jax import lax
from jax.sharding import PartitionSpec as P


def shards(gradient, right_panel, left_panel, second_moment):
    grad_float = gradient.astype(jnp.float32)
    whole_panel = lax.all_gather(right_panel, "wide", axis=1, tiled=True)
    partial_hidden = jnp.dot(
        grad_float, whole_panel, precision=lax.Precision.HIGHEST, preferred_element_type=jnp.float32
    )
    left_float = left_panel.astype(jnp.float32)
    contract = (((0,), (0,)), ((), ()))
    hidden_panel = lax.psum_scatter(partial_hidden, "narrow", scatter_dimension=1, tiled=True)
    partial_rotated = lax.dot_general(
        left_float,
        hidden_panel,
        contract,
        precision=lax.Precision.HIGHEST,
        preferred_element_type=jnp.float32,
    )
    rotated = lax.psum_scatter(partial_rotated, "wide", scatter_dimension=0, tiled=True)
    moment_new = 0.95 * second_moment + 0.05 * rotated * rotated
    step_update = rotated / (jnp.sqrt(moment_new) + 1e-08)
    return (moment_new, step_update)


def solution(mesh):
    placed = (P("wide", "narrow"), P("narrow", "wide"), P("wide", None), P("wide", "narrow"))
    return jax.shard_map(
        shards,
        mesh=mesh,
        in_specs=placed,
        out_specs=(P("wide", "narrow"), P("wide", "narrow")),
        check_vma=False,
    )
```

profile of v0, /device:TPU:1, one launch (start us, length us, event | category | flops | bytes accessed | tf_op | source)
XLA Modules:
  0.0 311.8 jit_solution(1228381957472434028)
XLA Ops:
  7.2 0.0 copy-start
  7.2 0.0 all-gather.2.cloned.1.call-start
  7.2 0.7 all-gather.2.cloned.1.call-update
  7.9 0.0 copy-start.1
  7.9 0.0 reduce-scatter.7.cloned.1.call-start
  8.0 129.3 %all-gather.2.cloned.1.call-done = f32[6656,512]{0,1:T(8,128)} async-done(((f32[6656,16]{0,1:T(8,128)}), f32[6656,512]{0,1:T(8,128)}) %all-gather.2.cloned.1.call-update) | async-done | bytes 13631504 | tf_op jit(solution)/shard_map/all_gather | solution.py:9
  137.3 15.9 %convolution_bitcast_fusion = f32[512,512]{1,0:T(8,128)} fusion(bf16[512,6656]{1,0:T(8,128)(2,1)} %param.4, f32[6656,512]{0,1:T(8,128)} %all-gather.2.cloned.1.call-done), kind=kOutput, calls=%fused_computation | convolution fusion | flops 20937965568 | bytes 21495808
  153.2 0.0 reduce-scatter.7.cloned.1.call-update
  153.2 0.0 reduce-scatter.9.cloned.1.call-start
  153.2 33.6 %reduce-scatter.7.cloned.1.call-done = f32[64,512]{1,0:T(8,128)} async-done(((f32[512,512]{1,0:T(8,128)}), f32[64,512]{1,0:T(8,128)}) %reduce-scatter.7.cloned.1.call-update) | async-done | bytes 131088
  186.8 0.0 copy-done
  186.8 1.6 convolution_bitcast_fusion.1
  188.4 1.0 copy.14
  189.4 0.0 reduce-scatter.9.cloned.1.call-update
  189.4 0.0 copy-done.1
  189.4 0.1 copy.9
  189.5 113.5 %reduce-scatter.9.cloned.1.call-done = f32[32,64]{1,0:T(8,128)} async-done(((f32[1024,64]{1,0:T(8,128)}), f32[32,64]{1,0:T(8,128)}) %reduce-scatter.9.cloned.1.call-update) | async-done | bytes 8208
  303.0 0.8 copy.15
  303.9 0.7 copy.11
  304.6 0.7 copy.10
  (1 shorter events, 0.0 us)
Async XLA Ops:
  7.2 179.7 %copy-start = (bf16[512,1024]{1,0:T(8,128)(2,1)S(1)}, bf16[512,1024]{1,0:T(8,128)(2,1)}, u32[]{:S(2)}) copy-start(bf16[512,1024]{1,0:T(8,128)(2,1)} %param.6) | copy-start | bytes 3145732
  7.2 130.1 %all-gather.2.cloned.1.call-start = ((), (), s32[]{:S(2)}) async-start(), calls=%async_computation.2 | async-start | bytes 14057472 | tf_op jit(solution)/shard_map/all_gather | solution.py:9
  7.9 181.5 %copy-start.1 = (f32[32,64]{1,0:T(8,128)S(1)}, f32[32,64]{1,0:T(8,128)}, u32[]{:S(2)}) copy-start(f32[32,64]{1,0:T(8,128)} %param.7) | copy-start | bytes 24580
  7.9 178.9 %reduce-scatter.7.cloned.1.call-start = ((), (), s32[]{:S(2)}) async-start(), calls=%async_computation.3 | async-start | bytes 1179648
  153.2 149.8 %reduce-scatter.9.cloned.1.call-start = ((), (), s32[]{:S(2)}) async-start(), calls=%async_computation.4 | async-start | bytes 540672
Sparse Core Ops, SparseCore 0:
  10.8 126.4 all-gather.1
  153.3 33.4 reduce-scatter.6
  190.8 112.1 reduce-scatter.8
where the time goes:
time: 316 us; the launch traced here: 312 us
  waiting for transfers between devices  277 us (88%)
  matrix products  17.5 us (6%)
  between operations  13.8 us (4%)
  local copies, waits for them, and re-layouts  3.25 us (1%)
    unnamed x5, waiting for transfers between devices  148 us
    all_gather x1, waiting for transfers between devices, shards(): whole_panel = lax.all_gather(right_panel, 'wide', axis=1, tiled=True)  129 us
    unnamed x1, matrix products  15.9 us
  transfers between devices with their start and end apart: 3, of which 3 were waited for; matrix products, arithmetic and copies ran while one was open for 0% of the time, Pallas kernels for 0%

commit v1 on v0

v1 whole, which is shorter than its diff:
```python
import functools

import jax
import jax.numpy as jnp
from jax import lax
from jax.experimental import pallas as pl
from jax.experimental.pallas import tpu as pltpu
from jax.sharding import PartitionSpec as P

MESH = pl.DeviceIdType.MESH
NT = (((1,), (1,)), ((), ()))
F32, BF16 = jnp.float32, jnp.bfloat16

FFL = 6656
ROWS = 512
LEFT = 1024
TILE = 128
SPLIT = 26 * TILE
A, B, A2 = 0, 1, 2
HALF_A = 14 * TILE
HALF_B = 12 * TILE


def lanes(s, way, kind):
    if kind == B:
        if s < 4:
            return SPLIT, FFL - SPLIT
        return (SPLIT, HALF_B) if way == 0 else (SPLIT + HALF_B, FFL - SPLIT - HALF_B)
    if s < 4:
        return 0, SPLIT
    return (0, HALF_A) if way == 0 else (HALF_A, SPLIT - HALF_A)


def unit(s, way, other):
    if s == 0:
        return other
    if s == 4:
        return 14 + other
    return 2 + (s - 1) * 4 + way * 2 + other


def kernel(
    rt_ref, g_ref, l_ref, sm_ref, mom_ref, step_ref,
    panel, grad, left, left_t, acc, hidden, parts, stack, rot, gathered,
    own_sem, g_sem, l_sem, z_send, z_recv, y_send, y_recv, s_send, s_recv,
    n_send, n_recv, w_send, w_recv,
):
    w, n = lax.axis_index("wide"), lax.axis_index("narrow")
    yh, z, core = w // 16, lax.rem(w // 2, 8), lax.rem(w, 2)

    def at(y_hi, zz, cc):
        return (y_hi * 16 + lax.rem(zz + 16, 8) * 2 + cc, n)

    ring = (at(yh, z + 1, core), at(yh, z - 1, core))
    across = at(1 - yh, z, core)
    sibling = at(yh, z, 1 - core)

    own = pltpu.make_async_copy(rt_ref, panel.at[pl.ds(core * 2, 2)], own_sem)
    own.start()
    load_g = pltpu.make_async_copy(g_ref, grad, g_sem)
    load_g.start()
    load_l = pltpu.make_async_copy(l_ref, left, l_sem)
    load_l.start()

    barrier = pltpu.get_barrier_semaphore()
    greet = [*ring, at(yh, z + 2, core), at(yh, z - 2, core), across, sibling]
    greet += [(w, lax.rem(n + i, 8)) for i in range(1, 8)]
    for device in greet:
        pl.semaphore_signal(barrier, inc=1, device_id=device, device_id_type=MESH)
    own.wait()
    pl.semaphore_wait(barrier, len(greet))

    def block(u, first, size):
        return panel.at[pl.ds(u * 4 + core * 2, 2), :, pl.ds(first, size)]

    def remote(src, dst, send, recv, device):
        return pltpu.make_async_remote_copy(
            src_ref=src, dst_ref=dst, send_sem=send, recv_sem=recv, device_id=device, device_id_type=MESH
        )

    started = []

    def start(copy):
        copy.start()
        started.append(copy)

    def along_z(s, way, kind):
        first, size = lanes(s, way, kind)
        other = int(kind == A2)
        which = way * 12 + (s - 1) * 3 + kind
        return remote(
            block(unit(s - 1, way, other), first, size),
            block(unit(s, way, other), first, size),
            z_send.at[which], z_recv.at[which], ring[way],
        )

    def along_y(s, way, kind):
        first, size = lanes(s, way, kind)
        which = int(kind == B) if s == 0 else 2 + (s - 1) * 2 + way
        return remote(
            block(unit(s, way, 0), first, size), block(unit(s, way, 1), first, size),
            y_send.at[which], y_recv.at[which], across,
        )

    def to_sibling(u, group, first=0, size=FFL, slot=0):
        part = block(u, first, size)
        start(remote(part, part, s_send.at[u + 2 * slot], s_recv.at[group], sibling))

    def wait_bytes(ref, sem):
        pltpu.make_async_copy(ref, ref, sem).wait()

    def multiply(first_block, blocks, first, size, step, fresh):
        rows = blocks * 8

        def body(i, carry):
            cols = pl.ds(pl.multiple_of(first + i * step, TILE), step)
            value = panel[pl.ds(first_block, blocks), :, cols].reshape(rows, step)
            high = value.astype(BF16)
            low = (value - high.astype(F32)).astype(BF16)
            both = jnp.concatenate([high, low], axis=0)
            acc[: 2 * rows] += lax.dot_general(both, grad[:, cols], NT, preferred_element_type=F32)
            return carry

        if fresh:
            acc[: 2 * rows] = jnp.zeros((2 * rows, ROWS), F32)
        lax.fori_loop(0, size // step, body, 0)

    def scatter(s, first_unit, units):
        rows = units * 32
        hidden[first_unit * 32 : first_unit * 32 + rows] = acc[:rows] + acc[rows : 2 * rows]
        for k in range(units):
            u, way, other = first_unit + k, (k // 2 if 0 < s < 4 else 0), k % 2
            zz = lax.rem(z + (s if way == 1 else -s) + 8, 8)
            keeper = (yh if other == 0 else 1 - yh) * 4 + zz // 2
            ahead = lax.rem(keeper - n + 8, 8)
            place = pl.ds(pl.multiple_of(lax.rem(zz, 2) * 32, 32), 32)

            @pl.when(ahead == 0)
            def _():
                parts[7, place, :] = hidden[u * 32 : u * 32 + 32]

            @pl.when(ahead != 0)
            def _():
                remote(
                    hidden.at[pl.ds(u * 32, 32)], parts.at[7 - ahead, place], n_send, n_recv, (w, keeper)
                ).start()

    def rotate():
        wait_bytes(parts.at[pl.ds(0, 7)], n_recv)
        total = parts[0]
        for i in range(1, 8):
            total = total + parts[i]
        high = total.astype(BF16)
        stack[:64] = high
        stack[64:] = (total - high.astype(F32)).astype(BF16)

        def body(i, carry):
            out = lax.dot_general(
                left_t[pl.ds(pl.multiple_of(i * 256, 256), 256), :], stack[...], NT, preferred_element_type=F32
            )
            out = out + pltpu.roll(out, 64, 1)
            out = out.reshape(8, 2, 16, 128)
            lane = lax.broadcasted_iota(jnp.int32, (8, 16, 128), 2)
            rot[pl.ds(i * 8, 8)] = jnp.where(lane < 64, out[:, 0], out[:, 1])
            return carry

        lax.fori_loop(0, 4, body, 0)

        def send(i, carry):
            target = lax.rem(w + i, 32)
            remote(rot.at[target], gathered.at[i - 1], w_send, w_recv, (target, n)).start()
            return carry

        lax.fori_loop(1, 32, send, 0)
        gathered[31] = rot[w]

    first_z = 2 * lax.rem(n, 4)

    def distance(a):
        there = lax.rem(z - a + 8, 8)
        return jnp.minimum(there, lax.rem(8 - there, 8))

    last_step = jnp.maximum(distance(first_z), distance(first_z + 1))

    start(along_y(0, 0, A))
    for way in (0, 1):
        start(along_z(1, way, B))
    to_sibling(0, 0)
    for way in (0, 1):
        start(along_z(1, way, A))
    start(along_y(0, 0, B))

    load_l.wait()

    def turn(i, carry):
        cols = pl.ds(pl.multiple_of(i * 256, 256), 256)
        left_t[cols, :] = left[:, cols].T
        return carry

    lax.fori_loop(0, 4, turn, 0)

    along_y(0, 0, A).wait_recv()
    for way in (0, 1):
        start(along_z(1, way, A2))

    def forward_b(s):
        for way in (0, 1):
            along_z(s, way, B).wait_recv()
            if s < 4:
                start(along_z(s + 1, way, B))
            start(along_y(s, way, B))

    def forward_a(s):
        for way in (0, 1):
            along_z(s, way, A).wait_recv()
            if s < 4:
                start(along_z(s + 1, way, A))
                to_sibling(unit(s, way, 0), s)

    def forward_a2(s):
        for way in (0, 1):
            along_z(s, way, A2).wait_recv()
            if s < 4:
                start(along_z(s + 1, way, A2))

    def settle_y(s):
        for way in (0, 1):
            along_y(s, way, B).wait_recv()
            if s < 4:
                to_sibling(unit(s, way, 1), s)

    def compute(s):
        wait_bytes(panel.at[pl.ds(0, 8)], s_recv.at[s])
        multiply(unit(s, 0, 0) * 4, 16, 0, FFL, 512, True)
        scatter(s, unit(s, 0, 0), 4)

    forward_b(1)
    along_y(0, 0, B).wait_recv()
    to_sibling(1, 0)
    forward_a(1)
    load_g.wait()
    wait_bytes(panel.at[pl.ds(0, 4)], s_recv.at[0])
    multiply(0, 8, 0, FFL, 512, True)
    scatter(0, 0, 2)
    forward_a2(1)
    settle_y(1)
    forward_b(2)
    compute(1)
    forward_a(2)
    forward_a2(2)
    settle_y(2)
    forward_b(3)
    compute(2)
    forward_a(3)

    @pl.when(last_step <= 2)
    def _():
        rotate()

    forward_a2(3)
    settle_y(3)
    forward_b(4)
    to_sibling(14, 4, SPLIT, FFL - SPLIT, 0)
    compute(3)
    forward_a(4)
    to_sibling(14, 5, 0, SPLIT, 1)
    settle_y(4)
    to_sibling(15, 4, SPLIT, FFL - SPLIT, 0)
    forward_a2(4)
    to_sibling(15, 5, 0, SPLIT, 1)
    wait_bytes(panel.at[pl.ds(0, 4), :, pl.ds(SPLIT, FFL - SPLIT)], s_recv.at[4])
    multiply(56, 8, SPLIT, FFL - SPLIT, 256, True)
    wait_bytes(panel.at[pl.ds(0, 4), :, pl.ds(0, SPLIT)], s_recv.at[5])
    multiply(56, 8, 0, SPLIT, 256, False)
    scatter(4, 14, 2)

    @pl.when(last_step > 2)
    def _():
        rotate()

    wait_bytes(gathered.at[pl.ds(0, 31)], w_recv)
    rotated = jnp.sum(gathered[...], axis=0)
    rotated = jnp.concatenate([rotated, pltpu.roll(rotated, 64, 1)], axis=0)[:, :64]
    moment = 0.95 * sm_ref[...] + 0.05 * rotated * rotated
    mom_ref[...] = moment
    step_ref[...] = rotated / (jnp.sqrt(moment) + 1e-08)

    for copy in started:
        copy.wait_send()
    wait_bytes(hidden.at[pl.ds(0, 448)], n_send)
    wait_bytes(gathered.at[pl.ds(0, 31)], w_send)


def shards(gradient, right_panel, left_panel, second_moment):
    panel_t = right_panel.T.reshape(2, 8, FFL)
    anywhere = pl.BlockSpec(memory_space=pl.ANY)
    vmem = pl.BlockSpec(memory_space=pltpu.VMEM)
    dma = pltpu.SemaphoreType.DMA
    return pl.pallas_call(
        kernel,
        out_shape=[jax.ShapeDtypeStruct(second_moment.shape, F32)] * 2,
        in_specs=[anywhere, anywhere, anywhere, vmem],
        out_specs=[vmem, vmem],
        scratch_shapes=[
            pltpu.VMEM((64, 8, FFL), F32),
            pltpu.VMEM((ROWS, FFL), BF16),
            pltpu.VMEM((ROWS, LEFT), BF16),
            pltpu.VMEM((LEFT, ROWS), BF16),
            pltpu.VMEM((256, ROWS), F32),
            pltpu.VMEM((512, ROWS), F32),
            pltpu.VMEM((8, 64, ROWS), F32),
            pltpu.VMEM((128, ROWS), BF16),
            pltpu.VMEM((32, 16, 128), F32),
            pltpu.VMEM((32, 16, 128), F32),
            dma, dma, dma, dma((24,)), dma((24,)), dma((10,)), dma((10,)), dma((18,)), dma((6,)),
            dma, dma, dma, dma,
        ],
        compiler_params=pltpu.CompilerParams(
            collective_id=0, has_side_effects=True, vmem_limit_bytes=60 * 2**20
        ),
    )(panel_t, gradient, left_panel, second_moment)


def solution(mesh):
    placed = (P("wide", "narrow"), P("narrow", "wide"), P("wide", None), P("wide", "narrow"))
    return jax.shard_map(
        shards,
        mesh=mesh,
        in_specs=placed,
        out_specs=(P("wide", "narrow"), P("wide", "narrow")),
        check_vma=False,
    )
```

time: 316 us -> 100 us (0.32); the launches traced: 312 us -> 99.8 us
  waiting for transfers between devices: 277 us -> 0 us
  Pallas kernels: 0 us -> 96.5 us
  matrix products: 17.5 us -> 0 us
  between operations: 13.8 us -> 0.64 us
    unnamed x5 -> x0, waiting for transfers between devices: 148 us -> none
    all_gather x1 -> x0, waiting for transfers between devices: 129 us -> none  [shards(): whole_panel = lax.all_gather(right_panel, 'wide', axis=1, tiled=True)]
    pallas_call x0 -> x1, Pallas kernels: none -> 96.5 us  [shards(): pl.pallas_call(kernel, out_shape=[jax.ShapeDtypeStruct(second_moment.shap...]
    unnamed x1 -> x0, matrix products: 15.9 us -> none
  transfers between devices with their start and end apart: 3 -> 0, of which waited for: 3 -> 0; matrix products, arithmetic and copies ran while one was open for 0% -> 0% of each run, Pallas kernels for 0% -> 0%
where the time goes in v1:
time: 100 us; the launch traced here: 99.8 us
  Pallas kernels  96.5 us (96%)
  local copies, waits for them, and re-layouts  2.65 us (3%)
    pallas_call x1, Pallas kernels, shards(): pl.pallas_call(kernel, out_shape=[jax.ShapeDtypeStruct(second_moment.shap...  96.5 us
    unnamed x2, local copies, waits for them, and re-layouts  2.65 us

profile of v1, /device:TPU:1, one launch (start us, length us, event | category | flops | bytes accessed | tf_op | source)
XLA Modules:
  0.0 99.8 jit_solution(9610139482662213778)
XLA Ops:
  0.6 96.5 %shard_map.59 = (f32[32,64]{1,0:T(8,128)}, f32[32,64]{1,0:T(8,128)}) custom-call(f32[2,8,6656]{2,1,0:T(8,128)} %bitcast.3, bf16[512,6656]{1,0:T(8,128)(2,1)} %g_ref.1, bf16[512,1024]{1,0:T(8,128)(2,1)} %l_ref.1, f32[32,64]{1,0:T(8,128)} %sm_ref.1), custom_call_target="tpu_custom_call" | custom-call | tf_op jit(solution)/shard_map/pallas_call | solution.py:299
  97.1 1.3 %copy.8 = f32[32,64]{1,0:T(8,128)} copy(f32[32,64]{1,0:T(8,128)} %get-tuple-element.4) | data formatting | bytes 16384
  98.5 1.3 %copy.9 = f32[32,64]{1,0:T(8,128)} copy(f32[32,64]{1,0:T(8,128)} %get-tuple-element.5) | data formatting | bytes 16384

commit v2 on v1

--- a/solution.py
+++ b/solution.py
@@ -15,10 +15,11 @@
 ROWS = 512
 LEFT = 1024
 TILE = 128
-SPLIT = 26 * TILE
+SPLIT = 24 * TILE
+DIRECT = 3
 A, B, A2 = 0, 1, 2
-HALF_A = 14 * TILE
-HALF_B = 12 * TILE
+HALF_A = 12 * TILE
+HALF_B = 14 * TILE
 
 
 def lanes(s, way, kind):
@@ -36,14 +37,16 @@
         return other
     if s == 4:
         return 14 + other
-    return 2 + (s - 1) * 4 + way * 2 + other
+    return 2 + (s - 1) * 4 + other * 2 + way
 
 
 def kernel(
     rt_ref, g_ref, l_ref, sm_ref, mom_ref, step_ref,
-    panel, grad, left, left_t, acc, hidden, parts, stack, rot, gathered,
+    panel, grad, left, left_t, acc, hidden, parts, x_parts, y_out, y_in, mine, stack,
+    rot, rot_in, gathered, last, last_in, last_gathered,
     own_sem, g_sem, l_sem, z_send, z_recv, y_send, y_recv, s_send, s_recv,
-    n_send, n_recv, w_send, w_recv,
+    n_send, n_recv, p_send, p_recv, x_recv, w_send, w_recv,
+    e_send, e_recv, q_send, q_recv,
 ):
     w, n = lax.axis_index("wide"), lax.axis_index("narrow")
     yh, z, core = w // 16, lax.rem(w // 2, 8), lax.rem(w, 2)
@@ -63,7 +66,7 @@
     load_l.start()
 
     barrier = pltpu.get_barrier_semaphore()
-    greet = [*ring, at(yh, z + 2, core), at(yh, z - 2, core), across, sibling]
+    greet = [*ring, across, sibling]
     greet += [(w, lax.rem(n + i, 8)) for i in range(1, 8)]
     for device in greet:
         pl.semaphore_signal(barrier, inc=1, device_id=device, device_id_type=MESH)
@@ -125,60 +128,190 @@
             acc[: 2 * rows] = jnp.zeros((2 * rows, ROWS), F32)
         lax.fori_loop(0, size // step, body, 0)
 
+    def hidden_copy(s, u):
+        way, other = (u % 2, (u - 2) % 4 // 2) if 0 < s < 4 else (0, u % 2)
+        zz = lax.rem(z + (s if way == 1 else -s) + 8, 8)
+        there = yh if other == 0 else 1 - yh
+        source = hidden.at[pl.ds(u * 32, 32)]
+        if s >= DIRECT:
+            keeper = there * 4 + zz // 2
+            ahead = lax.rem(keeper - n + 8, 8)
+            half = lax.rem(zz, 2)
+            return (
+                remote(source, parts.at[7 - ahead, half], n_send.at[u], n_recv.at[half], (w, keeper)),
+                source, parts.at[7, half], ahead,
+            )
+        keeper = there * 2 + zz // 4
+        ahead = lax.rem(keeper - n // 2 + 4, 4)
+        quarter = lax.rem(zz, 4)
+        device = (w, keeper * 2 + lax.rem(n, 2))
+        return (
+            remote(source, x_parts.at[3 - ahead, quarter], n_send.at[u], x_recv.at[quarter], device),
+            source, x_parts.at[3, quarter], ahead,
+        )
+
+    scattered = []
+
     def scatter(s, first_unit, units):
         rows = units * 32
         hidden[first_unit * 32 : first_unit * 32 + rows] = acc[:rows] + acc[rows : 2 * rows]
-        for k in range(units):
-            u, way, other = first_unit + k, (k // 2 if 0 < s < 4 else 0), k % 2
-            zz = lax.rem(z + (s if way == 1 else -s) + 8, 8)
-            keeper = (yh if other == 0 else 1 - yh) * 4 + zz // 2
-            ahead = lax.rem(keeper - n + 8, 8)
-            place = pl.ds(pl.multiple_of(lax.rem(zz, 2) * 32, 32), 32)
+        for u in range(first_unit, first_unit + units):
+            copy, source, here, ahead = hidden_copy(s, u)
+            scattered.append((s, u))
 
             @pl.when(ahead == 0)
             def _():
-                parts[7, place, :] = hidden[u * 32 : u * 32 + 32]
+                here[...] = source[...]
 
             @pl.when(ahead != 0)
             def _():
-                remote(
-                    hidden.at[pl.ds(u * 32, 32)], parts.at[7 - ahead, place], n_send, n_recv, (w, keeper)
-                ).start()
-
-    def rotate():
-        wait_bytes(parts.at[pl.ds(0, 7)], n_recv)
-        total = parts[0]
-        for i in range(1, 8):
-            total = total + parts[i]
+                copy.start()
+
+    def distance(a):
+        there = lax.rem(z - a + 8, 8)
+        return jnp.minimum(there, lax.rem(8 - there, 8))
+
+    x_first = 4 * lax.rem(n // 2, 2)
+    y_lo = lax.rem(n, 2)
+
+    def to_pair(q):
+        return remote(y_out.at[q % 2], y_in.at[q % 2], p_send.at[q % 2], p_recv.at[q % 2], (w, n + 1 - 2 * y_lo))
+
+    def reduce_x(s):
+        for q in range(4):
+
+            @pl.when(distance(x_first + q) == s)
+            def _():
+                wait_bytes(x_parts.at[pl.ds(0, 3), q], x_recv.at[q])
+                total = x_parts[0, q] + x_parts[1, q] + x_parts[2, q] + x_parts[3, q]
+
+                @pl.when(y_lo == q // 2)
+                def _():
+                    mine[q % 2] = total
+
+                @pl.when(y_lo != q // 2)
+                def _():
+                    y_out[q % 2] = total
+                    to_pair(q).start()
+
+    first_z = 2 * lax.rem(n, 4)
+
+    spot = w // 2
+
+    def fill_stack(total):
         high = total.astype(BF16)
         stack[:64] = high
         stack[64:] = (total - high.astype(F32)).astype(BF16)
 
+    def rotated_rows(i):
+        cols = pl.ds(pl.multiple_of(i * 256, 256), 256)
+        out = lax.dot_general(left_t[cols, :], stack[...], NT, preferred_element_type=F32)
+        return out + pltpu.roll(out, 64, 1)
+
+    swap_rot = remote(rot.at[1 - core], rot_in, e_send.at[0], e_recv.at[0], sibling)
+    swap_last = remote(last.at[1 - core], last_in, e_send.at[1], e_recv.at[1], sibling)
+
+    def rotate_start():
+        for half in (0, 1):
+            d = distance(first_z + half)
+
+            @pl.when(d == 4)
+            def _():
+                mine[half] = jnp.zeros((32, ROWS), F32)
+
+            @pl.when(d == DIRECT)
+            def _():
+                wait_bytes(parts.at[pl.ds(0, 7), half], n_recv.at[half])
+                total = parts[0, half]
+                for i in range(1, 8):
+                    total = total + parts[i, half]
+                mine[half] = total
+
+            @pl.when(d < DIRECT)
+            def _():
+                wait_bytes(y_in.at[half], p_recv.at[half])
+                mine[half] += y_in[half]
+
+        fill_stack(mine[...].reshape(64, ROWS))
+
         def body(i, carry):
-            out = lax.dot_general(
-                left_t[pl.ds(pl.multiple_of(i * 256, 256), 256), :], stack[...], NT, preferred_element_type=F32
-            )
-            out = out + pltpu.roll(out, 64, 1)
-            out = out.reshape(8, 2, 16, 128)
-            lane = lax.broadcasted_iota(jnp.int32, (8, 16, 128), 2)
-            rot[pl.ds(i * 8, 8)] = jnp.where(lane < 64, out[:, 0], out[:, 1])
+            out = rotated_rows(i).reshape(4, 2, 2, 16, 128)
+            lane = lax.broadcasted_iota(jnp.int32, (4, 16, 128), 2)
+            for c in (0, 1):
+                rot[c, pl.ds(i * 4, 4)] = jnp.where(lane < 64, out[:, c, 0], out[:, c, 1])
             return carry
 
         lax.fori_loop(0, 4, body, 0)
+        swap_rot.start()
+
+    def rotate_finish():
+        swap_rot.wait_recv()
+
+        def add(k, carry):
+            rot[core, k] += rot_in[k]
+            return carry
+
+        lax.fori_loop(0, 16, add, 0)
 
         def send(i, carry):
-            target = lax.rem(w + i, 32)
-            remote(rot.at[target], gathered.at[i - 1], w_send, w_recv, (target, n)).start()
-            return carry
-
-        lax.fori_loop(1, 32, send, 0)
-        gathered[31] = rot[w]
-
-    first_z = 2 * lax.rem(n, 4)
-
-    def distance(a):
-        there = lax.rem(z - a + 8, 8)
-        return jnp.minimum(there, lax.rem(8 - there, 8))
+            k = lax.rem(spot + i, 16)
+            remote(rot.at[core, k], gathered.at[i - 1], w_send, w_recv, (k * 2 + core, n)).start()
+            return carry
+
+        lax.fori_loop(1, 16, send, 0)
+        gathered[15] = rot[core, spot]
+
+    def last_start():
+        fill_stack(acc[:64] + acc[64:128])
+
+        def body(i, carry):
+            out = rotated_rows(i)
+            turned = pltpu.roll(out, 32, 1).reshape(4, 2, 4, 8, 128)
+            out = out.reshape(4, 2, 4, 8, 128)
+            which = lax.broadcasted_iota(jnp.int32, (4, 8, 128), 2) // 32
+            for c in (0, 1):
+                for other in (0, 1):
+                    even, odd = (out, turned) if other == 0 else (turned, out)
+                    value = jnp.where(which == 0, even[:, c, 0], odd[:, c, 1])
+                    value = jnp.where(which == 2, even[:, c, 2], value)
+                    last[c, pl.ds(i * 4, 4), other] = jnp.where(which == 3, odd[:, c, 3], value)
+            return carry
+
+        lax.fori_loop(0, 4, body, 0)
+        swap_last.start()
+
+    far_chip = lax.rem(z + 4, 8)
+    own_last = lax.rem(n, 4) == far_chip // 2
+
+    def last_finish():
+        swap_last.wait_recv()
+
+        def add(k, carry):
+            last[core, k] += last_in[k]
+            return carry
+
+        lax.fori_loop(0, 16, add, 0)
+        half = lax.rem(z, 2)
+        slot = half * 16 + yh * 8 + n
+
+        def send(i, carry):
+            k = lax.rem(spot + i, 16)
+            for other in (0, 1):
+                keeper = (yh if other == 0 else 1 - yh) * 4 + far_chip // 2
+                here = (k == spot) & (keeper == n)
+                source, target = last.at[core, k, other], last_gathered.at[slot]
+
+                @pl.when(here)
+                def _():
+                    pltpu.make_async_copy(source, target, q_recv.at[half]).start()
+
+                @pl.when(jnp.logical_not(here))
+                def _():
+                    remote(source, target, q_send, q_recv.at[half], (k * 2 + core, keeper)).start()
+
+            return carry
+
+        lax.fori_loop(0, 16, send, 0)
 
     last_step = jnp.maximum(distance(first_z), distance(first_z + 1))
 
@@ -227,68 +360,117 @@
         for way in (0, 1):
             along_y(s, way, B).wait_recv()
             if s < 4:
-                to_sibling(unit(s, way, 1), s)
+                to_sibling(unit(s, way, 1), 6 if s == 3 else s)
 
     def compute(s):
         wait_bytes(panel.at[pl.ds(0, 8)], s_recv.at[s])
-        multiply(unit(s, 0, 0) * 4, 16, 0, FFL, 512, True)
+        multiply(unit(s, 0, 0) * 4, 16, 0, FFL, 1664, True)
         scatter(s, unit(s, 0, 0), 4)
 
     forward_b(1)
+    forward_a(1)
     along_y(0, 0, B).wait_recv()
     to_sibling(1, 0)
-    forward_a(1)
     load_g.wait()
     wait_bytes(panel.at[pl.ds(0, 4)], s_recv.at[0])
-    multiply(0, 8, 0, FFL, 512, True)
+    multiply(0, 8, 0, FFL, 1664, True)
     scatter(0, 0, 2)
+    forward_b(2)
     forward_a2(1)
     settle_y(1)
-    forward_b(2)
+    forward_a(2)
     compute(1)
-    forward_a(2)
+    reduce_x(0)
+    forward_b(3)
     forward_a2(2)
     settle_y(2)
-    forward_b(3)
     compute(2)
+    reduce_x(1)
     forward_a(3)
+    forward_b(4)
+    to_sibling(14, 4, SPLIT, FFL - SPLIT, 0)
+    wait_bytes(panel.at[pl.ds(0, 4)], s_recv.at[3])
+    multiply(unit(3, 0, 0) * 4, 8, 0, FFL, 1664, True)
+    scatter(3, unit(3, 0, 0), 2)
+    reduce_x(2)
+    forward_a2(3)
+    settle_y(3)
+    wait_bytes(panel.at[pl.ds(0, 4)], s_recv.at[6])
+    multiply(unit(3, 0, 1) * 4, 8, 0, FFL, 1664, True)
+    scatter(3, unit(3, 0, 1), 2)
+    forward_a(4)
+    to_sibling(14, 5, 0, SPLIT, 1)
 
     @pl.when(last_step <= 2)
     def _():
-        rotate()
-
-    forward_a2(3)
-    settle_y(3)
-    forward_b(4)
-    to_sibling(14, 4, SPLIT, FFL - SPLIT, 0)
-    compute(3)
-    forward_a(4)
-    to_sibling(14, 5, 0, SPLIT, 1)
+        rotate_start()
+
+    forward_a2(4)
+    to_sibling(15, 5, 0, SPLIT, 1)
     settle_y(4)
     to_sibling(15, 4, SPLIT, FFL - SPLIT, 0)
-    forward_a2(4)
-    to_sibling(15, 5, 0, SPLIT, 1)
+    wait_bytes(panel.at[pl.ds(0, 4), :, pl.ds(0, SPLIT)], s_recv.at[5])
+    multiply(56, 8, 0, SPLIT, SPLIT // 2, True)
     wait_bytes(panel.at[pl.ds(0, 4), :, pl.ds(SPLIT, FFL - SPLIT)], s_recv.at[4])
-    multiply(56, 8, SPLIT, FFL - SPLIT, 256, True)
-    wait_bytes(panel.at[pl.ds(0, 4), :, pl.ds(0, SPLIT)], s_recv.at[5])
-    multiply(56, 8, 0, SPLIT, 256, False)
-    scatter(4, 14, 2)
+    multiply(56, 8, SPLIT, FFL - SPLIT, (FFL - SPLIT) // 2, False)
+    last_start()
+
+    @pl.when(last_step <= 2)
+    def _():
+        rotate_finish()
 
     @pl.when(last_step > 2)
     def _():
-        rotate()
-
-    wait_bytes(gathered.at[pl.ds(0, 31)], w_recv)
+        rotate_start()
+
+    last_finish()
+
+    @pl.when(last_step > 2)
+    def _():
+        rotate_finish()
+
+    wait_bytes(gathered.at[pl.ds(0, 15)], w_recv)
     rotated = jnp.sum(gathered[...], axis=0)
-    rotated = jnp.concatenate([rotated, pltpu.roll(rotated, 64, 1)], axis=0)[:, :64]
+    rotated = jnp.concatenate([rotated, pltpu.roll(rotated, 64, 1)], axis=0)
+    for half in (0, 1):
+        wait_bytes(last_gathered.at[pl.ds(0, 16)], q_recv.at[half])
+    lane = lax.broadcasted_iota(jnp.int32, (8, 128), 1)
+    sums = [jnp.sum(last_gathered[half * 16 : half * 16 + 16], axis=0) for half in (0, 1)]
+    rows = []
+    for b in range(4):
+        low, high = (pltpu.roll(sums[half], (128 + 32 * (half - b)) % 128, 1) for half in (0, 1))
+        rows.append(jnp.where(lane < 32, low, high))
+    rotated = (rotated + jnp.concatenate(rows, axis=0))[:, :64]
     moment = 0.95 * sm_ref[...] + 0.05 * rotated * rotated
     mom_ref[...] = moment
     step_ref[...] = rotated / (jnp.sqrt(moment) + 1e-08)
 
     for copy in started:
         copy.wait_send()
-    wait_bytes(hidden.at[pl.ds(0, 448)], n_send)
-    wait_bytes(gathered.at[pl.ds(0, 31)], w_send)
+    for s, u in scattered:
+        copy, _, _, ahead = hidden_copy(s, u)
+
+        @pl.when(ahead != 0)
+        def _():
+            copy.wait_send()
+
+    for q in range(4):
+
+        @pl.when((distance(x_first + q) < DIRECT) & (y_lo != q // 2))
+        def _():
+            to_pair(q).wait_send()
+
+    wait_bytes(gathered.at[pl.ds(0, 15)], w_send)
+    swap_rot.wait_send()
+    swap_last.wait_send()
+
+    @pl.when(own_last)
+    def _():
+        wait_bytes(last_gathered.at[pl.ds(0, 31)], q_send)
+
+    @pl.when(jnp.logical_not(own_last))
+    def _():
+        wait_bytes(last_gathered, q_send)
 
 
 def shards(gradient, right_panel, left_panel, second_moment):
@@ -308,12 +490,21 @@
             pltpu.VMEM((LEFT, ROWS), BF16),
             pltpu.VMEM((256, ROWS), F32),
             pltpu.VMEM((512, ROWS), F32),
-            pltpu.VMEM((8, 64, ROWS), F32),
+            pltpu.VMEM((8, 2, 32, ROWS), F32),
+            pltpu.VMEM((4, 4, 32, ROWS), F32),
+            pltpu.VMEM((2, 32, ROWS), F32),
+            pltpu.VMEM((2, 32, ROWS), F32),
+            pltpu.VMEM((2, 32, ROWS), F32),
             pltpu.VMEM((128, ROWS), BF16),
-            pltpu.VMEM((32, 16, 128), F32),
-            pltpu.VMEM((32, 16, 128), F32),
-            dma, dma, dma, dma((24,)), dma((24,)), dma((10,)), dma((10,)), dma((18,)), dma((6,)),
-            dma, dma, dma, dma,
+            pltpu.VMEM((2, 16, 16, 128), F32),
+            pltpu.VMEM((16, 16, 128), F32),
+            pltpu.VMEM((16, 16, 128), F32),
+            pltpu.VMEM((2, 16, 2, 8, 128), F32),
+            pltpu.VMEM((16, 2, 8, 128), F32),
+            pltpu.VMEM((32, 8, 128), F32),
+            dma, dma, dma, dma((24,)), dma((24,)), dma((10,)), dma((10,)), dma((18,)), dma((7,)),
+            dma((16,)), dma((2,)), dma((2,)), dma((2,)), dma((4,)), dma, dma,
+            dma((2,)), dma((2,)), dma, dma((2,)),
         ],
         compiler_params=pltpu.CompilerParams(
             collective_id=0, has_side_effects=True, vmem_limit_bytes=60 * 2**20

time: 100 us -> 84.9 us (0.85)
  Pallas kernels: 96.5 us -> 81.2 us
    pallas_call x1, Pallas kernels: 96.5 us -> 81.2 us  [shards(): pl.pallas_call(kernel, out_shape=[jax.ShapeDtypeStruct(second_moment.shap...]
where the time goes in v2:
time: 84.9 us; the launch traced here: 84.5 us
  Pallas kernels  81.2 us (96%)
  local copies, waits for them, and re-layouts  2.65 us (3%)
    pallas_call x1, Pallas kernels, shards(): pl.pallas_call(kernel, out_shape=[jax.ShapeDtypeStruct(second_moment.shap...  81.2 us
    unnamed x2, local copies, waits for them, and re-layouts  2.65 us

profile of v2, /device:TPU:1, one launch (start us, length us, event | category | flops | bytes accessed | tf_op | source)
XLA Modules:
  0.0 84.5 jit_solution(1736233689047854642)
XLA Ops:
  0.6 81.2 %shard_map.59 = (f32[32,64]{1,0:T(8,128)}, f32[32,64]{1,0:T(8,128)}) custom-call(f32[2,8,6656]{2,1,0:T(8,128)} %bitcast.3, bf16[512,6656]{1,0:T(8,128)(2,1)} %g_ref.1, bf16[512,1024]{1,0:T(8,128)(2,1)} %l_ref.1, f32[32,64]{1,0:T(8,128)} %sm_ref.1), custom_call_target="tpu_custom_call" | custom-call | tf_op jit(solution)/shard_map/pallas_call | solution.py:481
  81.8 1.3 %copy.8 = f32[32,64]{1,0:T(8,128)} copy(f32[32,64]{1,0:T(8,128)} %get-tuple-element.4) | data formatting | bytes 16384
  83.2 1.3 %copy.9 = f32[32,64]{1,0:T(8,128)} copy(f32[32,64]{1,0:T(8,128)} %get-tuple-element.5) | data formatting | bytes 16384

commit v3 on v2

--- a/solution.py
+++ b/solution.py
@@ -41,7 +41,7 @@
 
 
 def kernel(
-    rt_ref, g_ref, l_ref, sm_ref, mom_ref, step_ref,
+    rt_ref, g_ref, l_ref, out_ref,
     panel, grad, left, left_t, acc, hidden, parts, x_parts, y_out, y_in, mine, stack,
     rot, rot_in, gathered, last, last_in, last_gathered,
     own_sem, g_sem, l_sem, z_send, z_recv, y_send, y_recv, s_send, s_recv,
@@ -407,6 +407,11 @@
 
     forward_a2(4)
     to_sibling(15, 5, 0, SPLIT, 1)
+
+    @pl.when(last_step <= 2)
+    def _():
+        rotate_finish()
+
     settle_y(4)
     to_sibling(15, 4, SPLIT, FFL - SPLIT, 0)
     wait_bytes(panel.at[pl.ds(0, 4), :, pl.ds(0, SPLIT)], s_recv.at[5])
@@ -415,19 +420,30 @@
     multiply(56, 8, SPLIT, FFL - SPLIT, (FFL - SPLIT) // 2, False)
     last_start()
 
-    @pl.when(last_step <= 2)
-    def _():
-        rotate_finish()
+    last_finish()
 
     @pl.when(last_step > 2)
     def _():
         rotate_start()
 
-    last_finish()
-
     @pl.when(last_step > 2)
     def _():
         rotate_finish()
+
+    for copy in started:
+        copy.wait_send()
+    for s, u in scattered:
+        copy, _, _, ahead = hidden_copy(s, u)
+
+        @pl.when(ahead != 0)
+        def _():
+            copy.wait_send()
+
+    for q in range(4):
+
+        @pl.when((distance(x_first + q) < DIRECT) & (y_lo != q // 2))
+        def _():
+            to_pair(q).wait_send()
 
     wait_bytes(gathered.at[pl.ds(0, 15)], w_recv)
     rotated = jnp.sum(gathered[...], axis=0)
@@ -441,24 +457,7 @@
         low, high = (pltpu.roll(sums[half], (128 + 32 * (half - b)) % 128, 1) for half in (0, 1))
         rows.append(jnp.where(lane < 32, low, high))
     rotated = (rotated + jnp.concatenate(rows, axis=0))[:, :64]
-    moment = 0.95 * sm_ref[...] + 0.05 * rotated * rotated
-    mom_ref[...] = moment
-    step_ref[...] = rotated / (jnp.sqrt(moment) + 1e-08)
-
-    for copy in started:
-        copy.wait_send()
-    for s, u in scattered:
-        copy, _, _, ahead = hidden_copy(s, u)
-
-        @pl.when(ahead != 0)
-        def _():
-            copy.wait_send()
-
-    for q in range(4):
-
-        @pl.when((distance(x_first + q) < DIRECT) & (y_lo != q // 2))
-        def _():
-            to_pair(q).wait_send()
+    out_ref[...] = rotated
 
     wait_bytes(gathered.at[pl.ds(0, 15)], w_send)
     swap_rot.wait_send()
@@ -476,13 +475,12 @@
 def shards(gradient, right_panel, left_panel, second_moment):
     panel_t = right_panel.T.reshape(2, 8, FFL)
     anywhere = pl.BlockSpec(memory_space=pl.ANY)
-    vmem = pl.BlockSpec(memory_space=pltpu.VMEM)
     dma = pltpu.SemaphoreType.DMA
-    return pl.pallas_call(
+    rotated = pl.pallas_call(
         kernel,
-        out_shape=[jax.ShapeDtypeStruct(second_moment.shape, F32)] * 2,
-        in_specs=[anywhere, anywhere, anywhere, vmem],
-        out_specs=[vmem, vmem],
+        out_shape=jax.ShapeDtypeStruct(second_moment.shape, F32),
+        in_specs=[anywhere] * 3,
+        out_specs=pl.BlockSpec(memory_space=pltpu.VMEM),
         scratch_shapes=[
             pltpu.VMEM((64, 8, FFL), F32),
             pltpu.VMEM((ROWS, FFL), BF16),
@@ -509,7 +507,9 @@
         compiler_params=pltpu.CompilerParams(
             collective_id=0, has_side_effects=True, vmem_limit_bytes=60 * 2**20
         ),
-    )(panel_t, gradient, left_panel, second_moment)
+    )(panel_t, gradient, left_panel)
+    moment_new = 0.95 * second_moment + 0.05 * rotated * rotated
+    return moment_new, rotated / (jnp.sqrt(moment_new) + 1e-08)
 
 
 def solution(mesh):

time: 84.9 us -> 81 us (0.954)
  local copies, waits for them, and re-layouts: 2.65 us -> 0.01 us
  Pallas kernels: 81.2 us -> 78.8 us
  other arithmetic: 0 us -> 1.35 us
    unnamed x2, local copies, waits for them, and re-layouts: 2.65 us -> 0.01 us
    pallas_call x1, Pallas kernels: 81.2 us -> 78.8 us  [shards(): pl.pallas_call(kernel, out_shape=jax.ShapeDtypeStruct(second_moment.shape...]
    div x0 -> x1, other arithmetic: none -> 1.35 us  [shards(): return (moment_new, rotated / (jnp.sqrt(moment_new) + 1e-08))]
where the time goes in v3:
time: 81 us; the launch traced here: 80.8 us
  Pallas kernels  78.8 us (97%)
  other arithmetic  1.35 us (2%)
    pallas_call x1, Pallas kernels, shards(): pl.pallas_call(kernel, out_shape=jax.ShapeDtypeStruct(second_moment.shape...  78.8 us

profile of v3, /device:TPU:1, one launch (start us, length us, event | category | flops | bytes accessed | tf_op | source)
XLA Modules:
  0.0 80.8 jit_solution(8752376057399273841)
XLA Ops:
  0.6 0.0 copy-start
  0.6 78.8 %shard_map.59 = f32[32,64]{1,0:T(8,128)} custom-call(f32[2,8,6656]{2,1,0:T(8,128)} %bitcast.3, bf16[512,6656]{1,0:T(8,128)(2,1)} %g_ref.1, bf16[512,1024]{1,0:T(8,128)(2,1)} %l_ref.1), custom_call_target="tpu_custom_call" | custom-call | tf_op jit(solution)/shard_map/pallas_call | solution.py:479
  79.5 0.0 copy-done
  79.5 1.3 %add_divide_fusion = (f32[32,64]{1,0:T(8,128)}, f32[32,64]{1,0:T(8,128)}) fusion(f32[32,64]{1,0:T(8,128)} %shard_map.59, f32[32,64]{1,0:T(8,128)S(1)} %copy-done), kind=kLoop, calls=%fused_computation.2 | loop fusion | flops 12288 | bytes 32768 | tf_op jit(solution)/shard_map/div | solution.py:512
Async XLA Ops:
  0.6 78.8 %copy-start = (f32[32,64]{1,0:T(8,128)S(1)}, f32[32,64]{1,0:T(8,128)}, u32[]{:S(2)}) copy-start(f32[32,64]{1,0:T(8,128)} %param.7) | copy-start | bytes 24580

commit v4 on v3

--- a/solution.py
+++ b/solution.py
@@ -133,7 +133,7 @@
         zz = lax.rem(z + (s if way == 1 else -s) + 8, 8)
         there = yh if other == 0 else 1 - yh
         source = hidden.at[pl.ds(u * 32, 32)]
-        if s >= DIRECT:
+        if s == DIRECT and other == 1:
             keeper = there * 4 + zz // 2
             ahead = lax.rem(keeper - n + 8, 8)
             half = lax.rem(zz, 2)
@@ -171,6 +171,12 @@
         there = lax.rem(z - a + 8, 8)
         return jnp.minimum(there, lax.rem(8 - there, 8))
 
+    first_z = 2 * lax.rem(n, 4)
+    same_line = n // 4 == yh
+
+    def by_x(d):
+        return (d < DIRECT) | ((d == DIRECT) & same_line)
+
     x_first = 4 * lax.rem(n // 2, 2)
     y_lo = lax.rem(n, 2)
 
@@ -180,7 +186,7 @@
     def reduce_x(s):
         for q in range(4):
 
-            @pl.when(distance(x_first + q) == s)
+            @pl.when((distance(x_first + q) == s) & ((s < DIRECT) | same_line))
             def _():
                 wait_bytes(x_parts.at[pl.ds(0, 3), q], x_recv.at[q])
                 total = x_parts[0, q] + x_parts[1, q] + x_parts[2, q] + x_parts[3, q]
@@ -194,7 +200,6 @@
                     y_out[q % 2] = total
                     to_pair(q).start()
 
-    first_z = 2 * lax.rem(n, 4)
 
     spot = w // 2
 
@@ -219,7 +224,7 @@
             def _():
                 mine[half] = jnp.zeros((32, ROWS), F32)
 
-            @pl.when(d == DIRECT)
+            @pl.when((d == DIRECT) & jnp.logical_not(same_line))
             def _():
                 wait_bytes(parts.at[pl.ds(0, 7), half], n_recv.at[half])
                 total = parts[0, half]
@@ -227,7 +232,7 @@
                     total = total + parts[i, half]
                 mine[half] = total
 
-            @pl.when(d < DIRECT)
+            @pl.when(by_x(d))
             def _():
                 wait_bytes(y_in.at[half], p_recv.at[half])
                 mine[half] += y_in[half]
@@ -398,6 +403,7 @@
     wait_bytes(panel.at[pl.ds(0, 4)], s_recv.at[6])
     multiply(unit(3, 0, 1) * 4, 8, 0, FFL, 1664, True)
     scatter(3, unit(3, 0, 1), 2)
+    reduce_x(3)
     forward_a(4)
     to_sibling(14, 5, 0, SPLIT, 1)
 
@@ -441,7 +447,7 @@
 
     for q in range(4):
 
-        @pl.when((distance(x_first + q) < DIRECT) & (y_lo != q // 2))
+        @pl.when(by_x(distance(x_first + q)) & (y_lo != q // 2))
         def _():
             to_pair(q).wait_send()
 

time: 81 us -> 81 us (level)
  no operation moved by 1% of the time
where the time goes in v4:
time: 81 us; the launch traced here: 80.9 us
  Pallas kernels  78.9 us (97%)
  other arithmetic  1.35 us (2%)
    pallas_call x1, Pallas kernels, shards(): pl.pallas_call(kernel, out_shape=jax.ShapeDtypeStruct(second_moment.shape...  78.9 us

profile of v4, /device:TPU:1, one launch (start us, length us, event | category | flops | bytes accessed | tf_op | source)
XLA Modules:
  0.0 80.9 jit_solution(7878636344649780658)
XLA Ops:
  0.6 0.0 copy-start
  0.6 78.9 %shard_map.59 = f32[32,64]{1,0:T(8,128)} custom-call(f32[2,8,6656]{2,1,0:T(8,128)} %bitcast.3, bf16[512,6656]{1,0:T(8,128)(2,1)} %g_ref.1, bf16[512,1024]{1,0:T(8,128)(2,1)} %l_ref.1), custom_call_target="tpu_custom_call" | custom-call | tf_op jit(solution)/shard_map/pallas_call | solution.py:485
  79.5 0.0 copy-done
  79.5 1.3 %add_divide_fusion = (f32[32,64]{1,0:T(8,128)}, f32[32,64]{1,0:T(8,128)}) fusion(f32[32,64]{1,0:T(8,128)} %shard_map.59, f32[32,64]{1,0:T(8,128)S(1)} %copy-done), kind=kLoop, calls=%fused_computation.2 | loop fusion | flops 12288 | bytes 32768 | tf_op jit(solution)/shard_map/div | solution.py:518
Async XLA Ops:
  0.6 78.9 %copy-start = (f32[32,64]{1,0:T(8,128)S(1)}, f32[32,64]{1,0:T(8,128)}, u32[]{:S(2)}) copy-start(f32[32,64]{1,0:T(8,128)} %param.7) | copy-start | bytes 24580
